TPU v7x, 128 devices: a whole 4x4x4 slice. The times are simulated.
128 devices in a mesh: row: 8 (over y_lo, x), col: 16 (over y_hi, z, core).
Axes of the slice: x: 4, y: 4 (y_hi: 2, y_lo: 2; y = y_hi * 2 + y_lo), z: 4, core: 2. Of those that a mesh axis runs over, the one named last changes fastest.
Arguments:
- pair: float32 [512, 512, 128], P('row', 'col'), may hold values from -6 to 6
- single: bfloat16 [512, 384], P(('row', 'col')), may hold values from -6 to 6
- token_valid: int32 [512], replicated, may hold values 0 or 1
- chain_id: int32 [512], replicated, may hold values from 0 to 3, never falling along the last dimension, each value on 1 to 256 neighbouring positions
- w_tri_in: bfloat16 [128, 512], replicated, may hold values from -0.5 to 0.5
- w_tri_gate: bfloat16 [128, 128], replicated, may hold values from -0.5 to 0.5
- w_tri_out: bfloat16 [128, 128], replicated, may hold values from -0.5 to 0.5
- w_att_in: bfloat16 [128, 512], replicated, may hold values from -0.5 to 0.5
- w_att_bias: bfloat16 [128, 4], replicated, may hold values from -6 to 6
- w_att_out: bfloat16 [128, 128], replicated, may hold values from -0.5 to 0.5
- w_single_in: bfloat16 [384, 1536], replicated, may hold values from -0.3125 to 0.3125
- w_pair_bias: bfloat16 [128, 16], replicated, may hold values from -6 to 6
- w_single_out: bfloat16 [384, 384], replicated, may hold values from -0.3125 to 0.3125
Outputs:
- pair_out: float32 [512, 512, 128], P('row', 'col')
- single_out: float32 [512, 384], P(('row', 'col'))
All inputs are finite; a program needn't handle non-finite values.
Results may differ from a plain program's by a relative error of at most 0.034.
Values may be sent and summed in bfloat16 or wider, within the bound.
A program may use at most 128 MiB of HBM per device.

v0:
```python
import math

import jax
import jax.numpy as jnp
from jax import lax
from jax.sharding import PartitionSpec as P


def spread_2(value, axis, source):
    kept = jnp.where(lax.axis_index(axis) == source, value, 0).astype(value.dtype)
    return lax.psum(kept, axis)


def layer_norm(values):
    center = values - jnp.mean(values, axis=-1, keepdims=True)
    spread = jnp.mean(center * center, axis=-1, keepdims=True)
    return center * lax.rsqrt(spread + 1e-05)


def project(normed, weight):
    channel_width = normed.shape[-1]
    flat = jnp.dot(normed.reshape(-1, channel_width), weight, preferred_element_type=jnp.float32)
    return flat.reshape(normed.shape[:-1] + (weight.shape[1],))


def per_device(
    pair,
    single,
    token_valid,
    chain_id,
    w_tri_in,
    w_tri_gate,
    w_tri_out,
    w_att_in,
    w_att_bias,
    w_att_out,
    w_single_in,
    w_pair_bias,
    w_single_out,
):
    rows_blk, cols_blk, channels = pair.shape
    row_count = lax.axis_size("row")
    grand_total = rows_blk * row_count
    row_pos = lax.axis_index("row")
    col_pos = lax.axis_index("col")
    row_start = row_pos * rows_blk
    col_start = col_pos * cols_blk
    valid = token_valid.astype(jnp.float32)
    valid_rows = lax.dynamic_slice_in_dim(valid, row_start, rows_blk)
    valid_cols = lax.dynamic_slice_in_dim(valid, col_start, cols_blk)
    normed = layer_norm(pair).astype(jnp.bfloat16)
    tri_proj = project(normed, w_tri_in)
    pair_mask = (valid_rows[:, None] * valid_cols[None, :])[:, :, None]
    left = (
        jax.nn.sigmoid(tri_proj[..., 0:channels])
        * tri_proj[..., channels : 2 * channels]
        * pair_mask
    ).astype(jnp.bfloat16)
    right = (
        jax.nn.sigmoid(tri_proj[..., 2 * channels : 3 * channels])
        * tri_proj[..., 3 * channels : 4 * channels]
        * pair_mask
    ).astype(jnp.bfloat16)
    left_all, right_wide = (
        lax.all_gather(left, "col", axis=1, tiled=True),
        lax.all_gather(right, "col", axis=1, tiled=True),
    )
    owner = col_start // rows_blk
    offset = col_start - owner * rows_blk
    piece = lax.dynamic_slice_in_dim(right_wide, offset, cols_blk, 0)
    right_need = spread_2(piece, "row", owner)
    product = jnp.einsum("ikc,jkc->ijc", left_all, right_need, preferred_element_type=jnp.float32)
    gated = jax.nn.sigmoid(project(normed, w_tri_gate))
    after_mult = pair + gated * project(layer_norm(product).astype(jnp.bfloat16), w_tri_out)
    att_norm = layer_norm(after_mult).astype(jnp.bfloat16)
    att_proj = project(att_norm, w_att_in)
    heads = w_att_bias.shape[1]
    head_total = w_att_out.shape[0]
    head_dim = head_total // heads
    queries = (
        att_proj[..., 0:head_total]
        .astype(jnp.bfloat16)
        .reshape(rows_blk, cols_blk, heads, head_dim)
    )
    keys_local = att_proj[..., head_total : 2 * head_total].astype(jnp.bfloat16)
    values_local = att_proj[..., 2 * head_total : 3 * head_total].astype(jnp.bfloat16)
    att_gate = att_proj[..., 3 * head_total : 4 * head_total]
    tri_bias = project(att_norm, w_att_bias).reshape(rows_blk, cols_blk * heads)
    bias_wide = lax.all_gather(tri_bias, "col", axis=1, tiled=True)
    bias_full = lax.all_gather(bias_wide, "row", axis=0, tiled=True).reshape(
        grand_total, grand_total, heads
    )
    bias_mine = lax.dynamic_slice_in_dim(bias_full, row_start, rows_blk, 1)
    att_scale = 1.0 / math.sqrt(head_dim)
    start_peak = jnp.full((cols_blk, heads, rows_blk), -1e30, jnp.float32)
    peak = start_peak
    key_piece = lax.all_gather(keys_local, "row", axis=0, tiled=True)
    value_piece = lax.all_gather(values_local, "row", axis=0, tiled=True)
    span = key_piece.shape[0]
    key_heads = key_piece.reshape(span, cols_blk, heads, head_dim)
    value_heads = value_piece.reshape(span, cols_blk, heads, head_dim)
    logit_scores = (
        jnp.einsum("ijhd,kjhd->jhik", queries, key_heads, preferred_element_type=jnp.float32)
        * att_scale
    )
    logit_scores = logit_scores + jnp.transpose(bias_mine, (2, 1, 0))[None]
    logit_scores = logit_scores + (valid - 1.0) * 10000.0
    new_peak = jnp.maximum(peak, jnp.max(logit_scores, axis=-1))
    expo = jnp.exp(logit_scores - new_peak[..., None])
    mass = jnp.sum(expo, axis=-1)
    accum = jnp.einsum(
        "jhik,kjhd->jhid",
        expo.astype(jnp.bfloat16),
        value_heads,
        preferred_element_type=jnp.float32,
    )
    peak, mass, accum = (new_peak, mass, accum)
    attended = jnp.transpose(accum / mass[..., None], (2, 0, 1, 3)).reshape(
        rows_blk, cols_blk, head_total
    )
    tri_out = (jax.nn.sigmoid(att_gate) * attended).astype(jnp.bfloat16)
    pair_out = after_mult + project(tri_out, w_att_out)
    single_all = lax.all_gather(single, ("row", "col"), axis=0, tiled=True)
    own_rows = single.shape[0]
    channel_width = single.shape[1]
    single_head_count = w_pair_bias.shape[1]
    single_head_size = channel_width // single_head_count
    single_scale = 1.0 / math.sqrt(single_head_size)
    own_start = col_pos * own_rows
    query_src = lax.dynamic_slice_in_dim(single_all, row_start, rows_blk, 0)
    query_proj = project(
        layer_norm(query_src.astype(jnp.float32)).astype(jnp.bfloat16), w_single_in
    )
    single_query_rows = (
        query_proj[:, 0:channel_width]
        .astype(jnp.bfloat16)
        .reshape(rows_blk, single_head_count, single_head_size)
    )
    single_gate = query_proj[:, 3 * channel_width : 4 * channel_width]
    pair_bias = project(layer_norm(pair_out).astype(jnp.bfloat16), w_pair_bias)
    chain_rows = lax.dynamic_slice_in_dim(chain_id, row_start, rows_blk)
    bias_all = lax.all_gather(
        pair_bias.reshape(rows_blk, cols_blk * single_head_count), "col", axis=1, tiled=True
    )
    own_bias = lax.dynamic_slice_in_dim(
        bias_all.reshape(rows_blk, grand_total, single_head_count), own_start, own_rows, 0
    )
    key_projected = project(
        layer_norm(single_all.astype(jnp.float32)).astype(jnp.bfloat16), w_single_in
    )
    single_key_rows = (
        key_projected[:, channel_width : 2 * channel_width]
        .astype(jnp.bfloat16)
        .reshape(grand_total, single_head_count, single_head_size)
    )
    svalues = (
        key_projected[:, 2 * channel_width : 3 * channel_width]
        .astype(jnp.bfloat16)
        .reshape(grand_total, single_head_count, single_head_size)
    )
    local_query_rows = lax.dynamic_slice_in_dim(single_query_rows, own_start, own_rows, 0)
    own_chain = lax.dynamic_slice_in_dim(chain_rows, own_start, own_rows)
    allowed = (own_chain[:, None] == chain_id[None, :]) & (token_valid[None, :] == 1)
    mask_add = jnp.where(allowed, 0.0, -10000.0).astype(jnp.float32)
    logit_scores = (
        jnp.einsum(
            "abl,fbl->baf", local_query_rows, single_key_rows, preferred_element_type=jnp.float32
        )
        * single_scale
    )
    logit_scores = logit_scores + jnp.transpose(own_bias, (2, 0, 1)) + mask_add[None]
    full_peak = jnp.max(logit_scores, axis=-1, keepdims=True)
    expo = jnp.exp(logit_scores - full_peak)
    full_mass = jnp.sum(expo, axis=-1)
    full_accum = jnp.einsum(
        "hij,jhd->hid", expo.astype(jnp.bfloat16), svalues, preferred_element_type=jnp.float32
    )
    own_attended = jnp.transpose(full_accum / full_mass[..., None], (1, 0, 2)).reshape(
        own_rows, channel_width
    )
    own_gate = lax.dynamic_slice_in_dim(single_gate, own_start, own_rows, 0)
    gated_single = (jax.nn.sigmoid(own_gate) * own_attended).astype(jnp.bfloat16)
    single_out = single.astype(jnp.float32) + jnp.dot(
        gated_single, w_single_out, preferred_element_type=jnp.float32
    )
    return (pair_out, single_out)


def solution(mesh):
    placed = (
        P("row", "col", None),
        P(("row", "col"), None),
        P(),
        P(),
        P(),
        P(),
        P(),
        P(),
        P(),
        P(),
        P(),
        P(),
        P(),
    )
    return jax.shard_map(
        per_device,
        mesh=mesh,
        in_specs=placed,
        out_specs=(P("row", "col", None), P(("row", "col"), None)),
        check_vma=False,
    )
```

profile of v0, /device:TPU:1, one launch (start us, length us, event | category | flops | bytes accessed | tf_op | source)
XLA Modules:
  0.0 713.4 jit_solution(18177015660935794683)
XLA Ops:
  8.2 1.6 reduce_sum.126
  9.7 1.9 multiply_reduce_fusion.3
  11.7 2.1 fusion.34
  13.8 1.6 fusion.20
  16.2 80.2 %all-gather.8.cloned.1.call-done = bf16[64,512,128]{2,1,0:T(8,128)(2,1)} async-done(((bf16[64,32,128]{2,1,0:T(8,128)(2,1)}), bf16[64,512,128]{2,1,0:T(8,128)(2,1)}) %all-gather.8.cloned.1.call-update) | async-done | bytes 8388624 | tf_op jit(solution)/shard_map/all_gather | solution.py:66
  96.5 4.4 dynamic-slice_select_fusion
  101.1 72.9 %all-gather.10.cloned.1.call-done = bf16[64,512,128]{2,1,0:T(8,128)(2,1)} async-done(((bf16[64,32,128]{2,1,0:T(8,128)(2,1)}), bf16[64,512,128]{2,1,0:T(8,128)(2,1)}) %all-gather.10.cloned.1.call-update) | async-done | bytes 8388624 | tf_op jit(solution)/shard_map/all_gather | solution.py:65
  174.0 29.1 %copy.73 = bf16[64,512,128]{0,1,2:T(8,128)(2,1)} copy(bf16[64,512,128]{2,1,0:T(8,128)(2,1)} %all-gather.10.cloned.1.call-done) | data formatting | bytes 16777216 | tf_op jit(solution)/shard_map/all_gather | solution.py:65
  203.2 75.6 %all-reduce.2.cloned.1.call-done = bf16[32,512,128]{2,1,0:T(8,128)(2,1)} async-done(((bf16[32,512,128]{2,1,0:T(8,128)(2,1)}), bf16[32,512,128]{2,1,0:T(8,128)(2,1)}) %all-reduce.2.cloned.1.call-update) | async-done | bytes 4194320 | tf_op jit(solution)/shard_map/psum | solution.py:11
  278.8 7.9 %copy.72 = bf16[32,512,128]{1,0,2:T(8,128)(2,1)} copy(bf16[32,512,128]{2,1,0:T(8,128)(2,1)} %all-reduce.2.cloned.1.call-done) | data formatting | bytes 8388608 | tf_op jit(solution)/shard_map/psum | solution.py:11
  286.7 9.7 %bitcast_reduce_fusion = (f32[64,32]{0,1:T(8,128)S(1)}, f32[128,32,64]{2,1,0:T(8,128)S(1)}) fusion(bf16[32,512,128]{1,0,2:T(8,128)(2,1)} %copy.72, bf16[64,512,128]{0,1,2:T(8,128)(2,1)} %copy.73), kind=kOutput, calls=%fused_computation.10 | convolution fusion | flops 268695552 | bytes 13639680 | tf_op jit(solution)/shard_map/ikc,jkc->ijc/dot_general | solution.py:72
  298.3 2.8 copy.78
  301.4 2.5 fusion.76
  306.5 27.4 %all_gather.27 = f32[64,2048]{1,0:T(8,128)} all-gather(f32[64,128]{1,0:T(8,128)S(1)} %reshape_reshape.6), channel_id=1, replica_groups=mesh['row'=8,'col'=16] {'col'}, dimensions={1}, use_global_device_ids=true | all-gather | bytes 557056 | tf_op jit(solution)/shard_map/all_gather | solution.py:89
  333.9 2.6 fusion.77
  339.5 41.4 %all-gather.14.cloned.1.call-done = f32[512,2048]{1,0:T(8,128)} async-done(((f32[64,2048]{1,0:T(8,128)}), f32[512,2048]{1,0:T(8,128)}) %all-gather.14.cloned.1.call-update) | async-done | bytes 4194320 | tf_op jit(solution)/shard_map/all_gather | solution.py:90
  380.8 5.3 copy.82
  386.2 5.2 reshape.215
  392.6 41.1 %all-gather.12.cloned.1.call-done = bf16[512,32,128]{2,1,0:T(8,128)(2,1)} async-done(((bf16[64,32,128]{2,1,0:T(8,128)(2,1)}), bf16[512,32,128]{2,1,0:T(8,128)(2,1)}) %all-gather.12.cloned.1.call-update) | async-done | bytes 4194320 | tf_op jit(solution)/shard_map/all_gather | solution.py:97
  433.7 7.6 %copy.80 = bf16[512,32,128]{0,2,1:T(8,128)(2,1)} copy(bf16[512,32,128]{2,1,0:T(8,128)(2,1)} %all-gather.12.cloned.1.call-done) | data formatting | bytes 8388608 | tf_op jit(solution)/shard_map/all_gather | solution.py:97
  441.3 7.0 fusion.2
  448.3 5.7 copy-done.1
  454.0 4.7 fusion
  458.7 27.9 %all-gather.16.cloned.1.call-done = bf16[512,32,128]{2,1,0:T(8,128)(2,1)} async-done(((bf16[64,32,128]{2,1,0:T(8,128)(2,1)}), bf16[512,32,128]{2,1,0:T(8,128)(2,1)}) %all-gather.16.cloned.1.call-update) | async-done | bytes 4194320 | tf_op jit(solution)/shard_map/all_gather | solution.py:98
  486.6 7.6 %copy.84 = bf16[512,32,128]{0,2,1:T(8,128)(2,1)} copy(bf16[512,32,128]{2,1,0:T(8,128)(2,1)} %all-gather.16.cloned.1.call-done) | data formatting | bytes 8388608 | tf_op jit(solution)/shard_map/all_gather | solution.py:98
  494.2 10.6 %bitcast_divide_fusion = f32[64,32,4,32]{0,3,2,1:T(8,128)} fusion(bf16[512,32,4,32]{0,3,2,1:T(8,128)(2,1)} %bitcast.73, f32[32,4,64,512]{3,2,1,0:T(8,128)} %copy-done.1, f32[32,4,64]{2,1,0:T(4,128)S(1)} %broadcast_maximum_fusion, f32[512]{0:T(512)S(1)} %add_multiply_fusion, f32[4,64,512]{2,1,0:T(8,128)S(1)} %copy.83, f32[64,32,4]{0,2,1:T(4,128)S(1)} %bitcast.79), kind=kOutput, calls=%fused_computation.8 | convolution fusion | flops 289669120 | bytes 22611968 | tf_op jit(solution)/shard_map/jhik,kjhd->jhid/dot_general | solution.py:111
  504.8 2.5 copy.85
  507.4 2.1 fusion.78
  512.4 177.1 %all-gather = bf16[128,4,384]{2,1,0:T(4,128)(2,1)S(1)} all-gather(bf16[1,4,384]{2,1,0:T(4,128)(2,1)S(1)} %bitcast.80), channel_id=1, replica_groups=mesh['row'=8,'col'=16] {'row','col'}, dimensions={0}, use_global_device_ids=true | all-gather | bytes 396288 | tf_op jit(solution)/shard_map/all_gather | solution.py:123
  692.7 3.8 copy.90
  696.5 5.3 constant_dynamic-slice_fusion
  701.8 2.9 copy.97
  (104 shorter events, 18.9 us)
Async XLA Ops:
  7.2 682.7 %copy-start = (bf16[384,1536]{1,0:T(8,128)(2,1)S(1)}, bf16[384,1536]{1,0:T(8,128)(2,1)}, u32[]{:S(2)}) copy-start(bf16[384,1536]{1,0:T(8,128)(2,1)} %param.23) | copy-start | bytes 3538948
  7.2 89.3 %all-gather.8.cloned.1.call-start = ((), (), s32[]{:S(2)}) async-start(), calls=%async_computation | async-start | bytes 8912896 | tf_op jit(solution)/shard_map/all_gather | solution.py:66
  15.4 158.6 %all-gather.10.cloned.1.call-start = ((), (), s32[]{:S(2)}) async-start(), calls=%async_computation.2 | async-start | bytes 8912896 | tf_op jit(solution)/shard_map/all_gather | solution.py:65
  16.2 262.6 %all-reduce.2.cloned.1.call-start = ((), (), s32[]{:S(2)}) async-start(), calls=%async_computation.1 | async-start | bytes 8388608 | tf_op jit(solution)/shard_map/psum | solution.py:11
  100.9 279.9 %all-gather.14.cloned.1.call-start = ((), (), s32[]{:S(2)}) async-start(), calls=%async_computation.4 | async-start | bytes 4718592 | tf_op jit(solution)/shard_map/all_gather | solution.py:90
  296.4 4.8 copy-start.7
  296.5 4.9 copy-start.13
  301.4 4.1 copy-start.12
  303.9 1.0 copy-start.3
  304.0 30.0 %copy-start.6 = (bf16[128,512]{1,0:T(8,128)(2,1)S(1)}, bf16[128,512]{1,0:T(8,128)(2,1)}, u32[]{:S(2)}) copy-start(bf16[128,512]{1,0:T(8,128)(2,1)} %param.20) | copy-start | bytes 393220
  333.9 4.9 copy-start.8
  333.9 99.8 %all-gather.12.cloned.1.call-start = ((), (), s32[]{:S(2)}) async-start(), calls=%async_computation.3 | async-start | bytes 4718592 | tf_op jit(solution)/shard_map/all_gather | solution.py:97
  337.9 148.7 %all-gather.16.cloned.1.call-start = ((), (), s32[]{:S(2)}) async-start(), calls=%async_computation.5 | async-start | bytes 4718592 | tf_op jit(solution)/shard_map/all_gather | solution.py:98
  338.5 354.3 %all-gather.18.cloned.1.call-start = ((), (), s32[]{:S(2)}) async-start(), calls=%async_computation.6 | async-start | bytes 2228224 | tf_op jit(solution)/shard_map/all_gather | solution.py:142
  448.3 5.7 copy-start.1
  494.2 13.2 %copy-start.14 = (bf16[128,128]{1,0:T(8,128)(2,1)S(1)}, bf16[128,128]{1,0:T(8,128)(2,1)}, u32[]{:S(2)}) copy-start(bf16[128,128]{1,0:T(8,128)(2,1)} %param.22) | copy-start | bytes 98308
  507.3 3.4 copy-start.10
  509.4 180.8 %copy-start.2 = (f32[64,32,128]{2,1,0:T(8,128)}, f32[64,32,128]{2,1,0:T(8,128)S(1)}, u32[]{:S(2)}) copy-start(f32[64,32,128]{2,1,0:T(8,128)S(1)} %get-tuple-element.18) | copy-start | bytes 3145732
  509.4 2.9 copy-start.9
  690.2 0.8 copy-start.4
  690.2 2.3 copy-start.11
  701.8 4.0 slice-start
  701.8 4.0 copy-start.5
Sparse Core Ops, SparseCore 0:
  15.5 80.8 all-gather.7
  99.3 74.6 all-gather.9
  176.5 102.1 all-reduce.1
  334.0 46.7 all-gather.13
  382.3 51.3 all-gather.11
  435.2 51.3 all-gather.15
  512.5 46.8 all-gather.17
where the time goes:
time: 715 us; the launch traced here: 713 us
  waiting for transfers between devices  340 us (48%)
  blocking collectives  204 us (29%)
  local copies, waits for them, and re-layouts  92.8 us (13%)
  matrix products  40.3 us (6%)
  other arithmetic  20.1 us (3%)
  between operations  14.7 us (2%)
    all_gather x1, blocking collectives, per_device(): single_all = lax.all_gather(single, ('row', 'col'), axis=0, tiled=True)  177 us
    all_gather x1, waiting for transfers between devices, per_device(): lax.all_gather(right, 'col', axis=1, tiled=True)  80.2 us
    psum x1, waiting for transfers between devices, spread_2(): return lax.psum(kept, axis)  75.6 us
    all_gather x1, waiting for transfers between devices, per_device(): lax.all_gather(left, 'col', axis=1, tiled=True)  72.9 us
    all_gather x1, waiting for transfers between devices, per_device(): lax.all_gather(bias_wide, 'row', axis=0, tiled=True)  41.4 us
    all_gather x1, waiting for transfers between devices, per_device(): key_piece = lax.all_gather(keys_local, 'row', axis=0, tiled=True)  41.1 us
    all_gather x1, local copies, waits for them, and re-layouts, per_device(): lax.all_gather(left, 'col', axis=1, tiled=True)  29.1 us
    all_gather x1, waiting for transfers between devices, per_device(): value_piece = lax.all_gather(values_local, 'row', axis=0, tiled=True)  27.9 us
  transfers between devices with their start and end apart: 7, of which 6 were waited for; matrix products, arithmetic and copies ran while one was open for 10% of the time, Pallas kernels for 0%

commit v1 on v0

v1 whole, which is shorter than its diff:
```python
import math

import jax
import jax.numpy as jnp
from jax import lax
from jax.experimental import pallas as pl
from jax.experimental.pallas import tpu as pltpu
from jax.sharding import PartitionSpec as P

MESH = pl.DeviceIdType.MESH
F32 = jnp.float32
BF16 = jnp.bfloat16
ROWS = 8
COLS = 16
DEVICES = ROWS * COLS
LOG2E = math.log2(math.e)
EPS = 1e-05


def norm_down(values):
    mean = jnp.mean(values, axis=0, keepdims=True)
    center = values - mean
    spread = jnp.mean(center * center, axis=0, keepdims=True) + EPS
    return center * lax.rsqrt(spread), mean, jnp.sqrt(spread)


def norm_across(values):
    center = values - jnp.mean(values, axis=-1, keepdims=True)
    spread = jnp.mean(center * center, axis=-1, keepdims=True)
    return center * lax.rsqrt(spread + EPS)


def dot(a, b):
    return jnp.dot(a, b, preferred_element_type=F32)


def join_halves(a, b, half):
    first = lax.broadcasted_iota(jnp.int32, a.shape, 1) < 64
    if half == 0:
        return jnp.where(first, a, pltpu.roll(b, 64, 1))
    return jnp.where(first, pltpu.roll(a, 64, 1), b)


def pair_kernel(
    pair_ref,
    single_ref,
    valid_ref,
    chain_ref,
    valid_smem,
    chain_smem,
    w_tri_in_ref,
    w_tri_gate_ref,
    w_tri_out_ref,
    w_att_in_ref,
    w_att_bias_ref,
    w_att_out_ref,
    w_pair_bias_ref,
    w_single_in_ref,
    w_single_out_ref,
    out_ref,
    single_out_ref,
    w_in_t,
    w_gate_t,
    w_out_t,
    w_key_t,
    scr_a,
    scr_b,
    lr_send,
    lr_recv,
    norm_send,
    norm_recv,
    stat_send,
    stat_recv,
    prod_send,
    prod_recv,
    bias_send,
    bias_recv,
    bias_full,
    query_scr,
    key_scr,
    value_scr,
    gate_scr,
    delta_scr,
    delta_send,
    delta_recv,
    pb_send,
    pb_recv,
    single_send,
    single_recv,
    single_scr,
    single_keys,
    single_values,
    lr_sems,
    norm_sems,
    stat_sems,
    prod_sems,
    bias_sems,
    delta_sems,
    pb_sems,
    single_sems,
):
    row, col = lax.axis_index("row"), lax.axis_index("col")
    me = row * COLS + col
    group = col * ROWS + row

    barrier = pltpu.get_barrier_semaphore()

    def greet(step, carry):
        peer = lax.rem(me + step, DEVICES)
        pl.semaphore_signal(
            barrier,
            inc=1,
            device_id=(peer // COLS, lax.rem(peer, COLS)),
            device_id_type=MESH,
        )
        return carry

    lax.fori_loop(1, DEVICES, greet, 0)

    w_in_t[...] = jnp.transpose(w_tri_in_ref[...].astype(F32)).astype(BF16)
    w_gate_t[...] = jnp.transpose(w_tri_gate_ref[...].astype(F32)).astype(BF16)
    w_out_t[...] = jnp.transpose(w_tri_out_ref[...].astype(F32)).astype(BF16)
    w_key_t[...] = jnp.transpose(w_att_in_ref[:, 128:256].astype(F32)).astype(BF16)

    lane = lax.broadcasted_iota(jnp.int32, (1, 128), 1)
    valid_pick = valid_ref[pl.ds(row // 2, 1), :].astype(F32)
    valid_row = jnp.where(
        (lane // 64) == lax.rem(row, 2), valid_pick, pltpu.roll(valid_pick, 64, 1)
    )
    for t in range(3):
        single_scr[4 * t : 4 * t + 4, :] = single_ref[:, 128 * t : 128 * t + 128].astype(F32)
    single_scr[12:16, :] = jnp.zeros((4, 128), F32)
    single_send[...] = single_scr[0:16, :].astype(BF16)

    def project_block(step, carry):
        picks = [pair_ref[pl.ds(4 * step + a, 64, stride=32), :] for a in range(4)]
        turned = jnp.transpose(jnp.concatenate(picks, axis=0))
        normed, mean, deviation = norm_down(turned)
        normed = normed.astype(BF16)
        norm_send[step] = normed
        stat_send[step] = jnp.concatenate(
            [jnp.broadcast_to(mean, (4, 256)), jnp.broadcast_to(deviation, (4, 256))], axis=0
        )
        proj = dot(w_in_t[...], normed)
        masks = []
        for s in range(2):
            at = col * 32 + 4 * step + 2 * s
            pick = jnp.where(lane < 64, valid_smem[at], valid_smem[at + 1])
            masks.append(valid_row * pick.astype(F32))
        mask = jnp.concatenate(masks, axis=1)
        left = jax.nn.sigmoid(proj[0:128]) * proj[128:256] * mask
        right = jax.nn.sigmoid(proj[256:384]) * proj[384:512] * mask
        for s in range(2):
            scr_a[pl.ds(2 * step + s, 128, stride=16), :] = left[:, s * 128 : (s + 1) * 128]
            scr_b[pl.ds(2 * step + s, 128, stride=16), :] = right[:, s * 128 : (s + 1) * 128]
        return carry

    lax.fori_loop(0, 8, project_block, 0)
    lr_send[:, 0:16, :] = scr_a[...].reshape(128, 16, 128).astype(BF16)
    lr_send[:, 16:32, :] = scr_b[...].reshape(128, 16, 128).astype(BF16)

    pl.semaphore_wait(barrier, DEVICES - 1)

    def send_lr(step, carry):
        peer = lax.rem(me + step, DEVICES)
        pltpu.make_async_remote_copy(
            src_ref=lr_send.at[peer],
            dst_ref=lr_recv.at[me],
            send_sem=lr_sems.at[0],
            recv_sem=lr_sems.at[1],
            device_id=(peer // COLS, lax.rem(peer, COLS)),
            device_id_type=MESH,
        ).start()
        return carry

    lax.fori_loop(1, DEVICES, send_lr, 0)
    lr_recv[pl.ds(me, 1)] = lr_send[pl.ds(me, 1)]

    def send_single(step, carry):
        peer = lax.rem(me + step, DEVICES)
        pltpu.make_async_remote_copy(
            src_ref=single_send,
            dst_ref=single_recv.at[me],
            send_sem=single_sems.at[0],
            recv_sem=single_sems.at[1],
            device_id=(peer // COLS, lax.rem(peer, COLS)),
            device_id_type=MESH,
        ).start()
        return carry

    lax.fori_loop(1, DEVICES, send_single, 0)
    single_recv[me] = single_send[...]

    def send_norm(step, carry):
        peer = lax.rem(row + step, ROWS)
        for sent, received, sems in (
            (norm_send, norm_recv, norm_sems),
            (stat_send, stat_recv, stat_sems),
        ):
            pltpu.make_async_remote_copy(
                src_ref=sent.at[peer],
                dst_ref=received.at[row],
                send_sem=sems.at[0],
                recv_sem=sems.at[1],
                device_id=(peer, col),
                device_id_type=MESH,
            ).start()
        return carry

    lax.fori_loop(1, ROWS, send_norm, 0)
    norm_recv[pl.ds(row, 1)] = norm_send[pl.ds(row, 1)]
    stat_recv[pl.ds(row, 1)] = stat_send[pl.ds(row, 1)]

    rest = pl.ds(0, DEVICES - 1)
    pltpu.make_async_copy(lr_send.at[rest], lr_recv.at[rest], lr_sems.at[1]).wait()
    left_halves, right_halves = [[], []], [[], []]
    for q in range(4):
        for half in range(2):
            for halves, first in ((left_halves, 0), (right_halves, 16)):
                a = lr_recv[32 * q : 32 * q + 16, first : first + 16, :].reshape(256, 128)
                b = lr_recv[32 * q + 16 : 32 * q + 32, first : first + 16, :].reshape(256, 128)
                halves[half].append(join_halves(a.astype(F32), b.astype(F32), half))
    left_t = jnp.concatenate(
        [jnp.concatenate(left_halves[h], axis=1) for h in range(2)], axis=0
    ).astype(BF16)
    right_t = jnp.concatenate(
        [jnp.concatenate(right_halves[h], axis=1) for h in range(2)], axis=0
    )
    right_all = jnp.transpose(right_t).astype(BF16)
    product = dot(right_all, left_t)
    for ib in range(4):
        scr_a[pl.ds(ib, 512, stride=4), :] = product[:, ib * 128 : (ib + 1) * 128]
    prod_send[...] = scr_a[...].reshape(128, 16, 128).astype(BF16)

    def send_product(step, carry):
        peer = lax.rem(me + step, DEVICES)
        peer_row, peer_col = peer // COLS, lax.rem(peer, COLS)
        pltpu.make_async_remote_copy(
            src_ref=prod_send.at[peer_col * ROWS + peer_row],
            dst_ref=prod_recv.at[me],
            send_sem=prod_sems.at[0],
            recv_sem=prod_sems.at[1],
            device_id=(peer_row, peer_col),
            device_id_type=MESH,
        ).start()
        return carry

    lax.fori_loop(1, DEVICES, send_product, 0)
    prod_recv[pl.ds(me, 1)] = prod_send[pl.ds(group, 1)]

    seven = pl.ds(0, ROWS - 1)
    pltpu.make_async_copy(norm_send.at[seven], norm_recv.at[seven], norm_sems.at[1]).wait()
    pltpu.make_async_copy(stat_send.at[seven], stat_recv.at[seven], stat_sems.at[1]).wait()
    pltpu.make_async_copy(prod_send.at[rest], prod_recv.at[rest], prod_sems.at[1]).wait()

    scr_b[...] = prod_recv[...].reshape(2048, 128).astype(F32)
    w_qvg = jnp.concatenate(
        [w_att_in_ref[:, 0:128], w_att_in_ref[:, 256:512]], axis=1
    )
    valid_all = jnp.concatenate([valid_ref[a : a + 1, :] for a in range(4)], axis=1)
    key_mask = (valid_all.astype(F32) - 1.0) * 10000.0
    for jj in range(4):
        at = slice(64 * (jj // 2) * 2, 64 * (jj // 2) * 2 + 128)
        half = jj % 2
        normed = jnp.concatenate(
            [
                join_halves(
                    norm_recv[2 * ib, :, at].astype(F32),
                    norm_recv[2 * ib + 1, :, at].astype(F32),
                    half,
                )
                for ib in range(4)
            ],
            axis=1,
        )
        stats = jnp.concatenate(
            [
                join_halves(stat_recv[2 * ib, :, at], stat_recv[2 * ib + 1, :, at], half)
                for ib in range(4)
            ],
            axis=1,
        )
        received = jnp.concatenate(
            [scr_b[pl.ds(4 * jj + ib, 128, stride=16), :] for ib in range(4)], axis=1
        )
        product_norm, _, _ = norm_down(received)
        gate = jax.nn.sigmoid(dot(w_gate_t[...], normed.astype(BF16)))
        change = gate * dot(w_out_t[...], product_norm.astype(BF16))
        after = normed * stats[4:5] + stats[0:1] + change
        att_t, _, _ = norm_down(after)
        att_bf = att_t.astype(BF16)
        bias = lax.dot_general(
            w_att_bias_ref[...], att_bf, (((1,), (0,)), ((), ())), preferred_element_type=F32
        )
        bias = bias + key_mask
        bias = (bias - jnp.max(bias, axis=1, keepdims=True)) * LOG2E
        for kb in range(4):
            scr_a[pl.ds(4 * jj + kb, 4, stride=16), :] = bias[0:4, kb * 128 : (kb + 1) * 128]
        key_scr[jj] = dot(w_key_t[...], att_bf).astype(BF16)
        att_tok = jnp.transpose(att_t).astype(BF16)
        qvg = dot(att_tok, w_qvg)
        query_scr[jj] = (qvg[:, 0:128] * (LOG2E / math.sqrt(32.0))).astype(BF16)
        value_scr[jj, :, 0:128] = qvg[:, 128:256].astype(BF16)
        value_scr[jj, :, 128:256] = jnp.ones((512, 128), BF16)
        gate_scr[jj] = jax.nn.sigmoid(qvg[:, 256:384])
        delta_scr[jj] = jnp.transpose(change)
    bias_send[...] = scr_a[0:64, :].astype(BF16)

    def send_bias(step, carry):
        peer = lax.rem(me + step, DEVICES)
        pltpu.make_async_remote_copy(
            src_ref=bias_send,
            dst_ref=bias_recv.at[group],
            send_sem=bias_sems.at[0],
            recv_sem=bias_sems.at[1],
            device_id=(peer // COLS, lax.rem(peer, COLS)),
            device_id_type=MESH,
        ).start()
        return carry

    lax.fori_loop(1, DEVICES, send_bias, 0)
    bias_recv[group] = bias_send[...]

    pltpu.make_async_copy(single_recv.at[rest], single_recv.at[rest], single_sems.at[1]).wait()
    scr_b[...] = single_recv[...].reshape(2048, 128).astype(F32)
    for t in range(3):
        for a in range(4):
            single_scr[pl.ds(512 * t + a, 128, stride=4), :] = scr_b[
                pl.ds(4 * t + a, 128, stride=16), :
            ]
    single_all = jnp.concatenate(
        [single_scr[512 * t : 512 * t + 512, :] for t in range(3)], axis=1
    )
    single_norm = norm_across(single_all).astype(BF16)
    single_keys[...] = dot(single_norm, w_single_in_ref[:, 384:768]).astype(BF16)
    single_values[...] = dot(single_norm, w_single_in_ref[:, 768:1152]).astype(BF16)

    pltpu.make_async_copy(bias_recv.at[rest], bias_recv.at[rest], bias_sems.at[1]).wait()

    for h in range(4):
        scr_b[...] = bias_recv[:, 16 * h : 16 * h + 16, :].reshape(2048, 128).astype(F32)
        for kb in range(4):
            bias_full[h, :, kb * 128 : (kb + 1) * 128] = scr_b[pl.ds(kb, 512, stride=4), :]

    def attend(jj, carry):
        keys = key_scr[jj]
        down = lax.broadcasted_iota(jnp.int32, (128, 512), 0)
        head_keys = [
            jnp.where((down >= 32 * h) & (down < 32 * h + 32), keys.astype(F32), 0.0).astype(BF16)
            for h in range(4)
        ]
        across = lax.broadcasted_iota(jnp.int32, (128, 128), 1)
        for ib in range(4):
            span = slice(128 * ib, 128 * ib + 128)
            queries = query_scr[jj, span, :]
            attended = jnp.zeros((128, 128), F32)
            for h in range(4):
                scores = dot(queries, head_keys[h]) + bias_full[h, span, :]
                weights = jnp.exp2(scores - jnp.max(scores, axis=1, keepdims=True)).astype(BF16)
                summed = dot(weights, value_scr[jj])
                attended = jnp.where(
                    (across >= 32 * h) & (across < 32 * h + 32),
                    summed[:, 0:128] / summed[:, 128:256],
                    attended,
                )
            tri_out = (gate_scr[jj, span, :] * attended).astype(BF16)
            delta = delta_scr[jj, span, :] + dot(tri_out, w_att_out_ref[...])
            delta = delta.astype(BF16)
            delta_send[2 * ib, pl.ds(jj, 1)] = delta[0:64].reshape(1, 64, 128)
            delta_send[2 * ib + 1, pl.ds(jj, 1)] = delta[64:128].reshape(1, 64, 128)

        def send_delta(step, carry):
            peer = lax.rem(row + step, ROWS)
            pltpu.make_async_remote_copy(
                src_ref=delta_send.at[peer, jj],
                dst_ref=delta_recv.at[row, jj],
                send_sem=delta_sems.at[0],
                recv_sem=delta_sems.at[1],
                device_id=(peer, col),
                device_id_type=MESH,
            ).start()
            return carry

        lax.fori_loop(1, ROWS, send_delta, 0)
        return carry

    lax.fori_loop(0, 4, attend, 0)
    delta_recv[pl.ds(row, 1)] = delta_send[pl.ds(row, 1)]
    pltpu.make_async_copy(delta_send.at[seven], delta_recv.at[seven], delta_sems.at[1]).wait()

    def finish(step, carry):
        for jj in range(4):
            at = pl.ds(4 * step + jj, 64, stride=32)
            out_ref[at, :] = pair_ref[at, :] + delta_recv[step, jj].astype(F32)
        return carry

    lax.fori_loop(0, 8, finish, 0)

    def pair_bias(step, carry):
        normed = norm_across(out_ref[pl.ds(pl.multiple_of(256 * step, 256), 256), :]).astype(BF16)
        bias = lax.dot_general(
            w_pair_bias_ref[...], normed, (((1,), (1,)), ((), ())), preferred_element_type=F32
        )
        for s in range(2):
            pb_send[2 * step + s] = bias[:, 128 * s : 128 * s + 128]
        return carry

    lax.fori_loop(0, 8, pair_bias, 0)

    def send_pb(step, carry):
        peer = lax.rem(col + step, COLS)
        pltpu.make_async_remote_copy(
            src_ref=pb_send.at[peer],
            dst_ref=pb_recv.at[col],
            send_sem=pb_sems.at[0],
            recv_sem=pb_sems.at[1],
            device_id=(row, peer),
            device_id_type=MESH,
        ).start()
        return carry

    lax.fori_loop(1, COLS, send_pb, 0)
    pb_recv[pl.ds(col, 1)] = pb_send[pl.ds(col, 1)]
    fifteen = pl.ds(0, COLS - 1)
    pltpu.make_async_copy(pb_send.at[fifteen], pb_recv.at[fifteen], pb_sems.at[1]).wait()

    chain_all = jnp.concatenate([chain_ref[a : a + 1, :] for a in range(4)], axis=1)
    own = single_ref[...].astype(F32)
    own_norm = norm_across(own).astype(BF16)
    queries = dot(own_norm, w_single_in_ref[:, 0:384]).astype(BF16).astype(F32)
    gate = jax.nn.sigmoid(dot(own_norm, w_single_in_ref[:, 1152:1536]))
    head = lax.broadcasted_iota(jnp.int32, (16, 384), 0) * 24
    channel = lax.broadcasted_iota(jnp.int32, (16, 384), 1)
    mine = (channel >= head) & (channel < head + 24)
    stacked = jnp.concatenate(
        [jnp.where(mine, jnp.broadcast_to(queries[a : a + 1], (16, 384)), 0.0) for a in range(4)],
        axis=0,
    ).astype(BF16)
    scores = lax.dot_general(
        stacked, single_keys[...], (((1,), (1,)), ((), ())), preferred_element_type=F32
    ) * (1.0 / math.sqrt(24.0))
    quarter = lax.broadcasted_iota(jnp.int32, (16, 128), 1) // 32
    bias_rows = []
    for a in range(4):
        tiles = []
        for g in range(4):
            tile = jnp.zeros((16, 128), F32)
            for part in range(4):
                piece = pb_recv[4 * g + part]
                shift = (32 * (part - a)) % 128
                if shift:
                    piece = pltpu.roll(piece, shift, 1)
                tile = jnp.where(quarter == part, piece, tile)
            tiles.append(tile)
        allowed = (chain_all == chain_smem[4 * me + a]) & (valid_all == 1)
        bias_rows.append(jnp.concatenate(tiles, axis=1) + jnp.where(allowed, 0.0, -10000.0))
    scores = scores + jnp.concatenate(bias_rows, axis=0)
    expo = jnp.exp(scores - jnp.max(scores, axis=1, keepdims=True))
    mass = jnp.sum(expo, axis=1, keepdims=True)
    summed = dot(expo.astype(BF16), single_values[...]) / mass
    attended = jnp.concatenate(
        [
            jnp.sum(jnp.where(mine, summed[16 * a : 16 * a + 16], 0.0), axis=0, keepdims=True)
            for a in range(4)
        ],
        axis=0,
    )
    single_out_ref[...] = own + dot((gate * attended).astype(BF16), w_single_out_ref[...])

    pltpu.make_async_copy(lr_send.at[rest], lr_recv.at[rest], lr_sems.at[0]).wait()
    pltpu.make_async_copy(norm_send.at[seven], norm_recv.at[seven], norm_sems.at[0]).wait()
    pltpu.make_async_copy(stat_send.at[seven], stat_recv.at[seven], stat_sems.at[0]).wait()
    pltpu.make_async_copy(prod_send.at[rest], prod_recv.at[rest], prod_sems.at[0]).wait()
    pltpu.make_async_copy(bias_recv.at[rest], bias_recv.at[rest], bias_sems.at[0]).wait()
    pltpu.make_async_copy(delta_send.at[seven], delta_recv.at[seven], delta_sems.at[0]).wait()
    pltpu.make_async_copy(pb_send.at[fifteen], pb_recv.at[fifteen], pb_sems.at[0]).wait()
    pltpu.make_async_copy(single_recv.at[rest], single_recv.at[rest], single_sems.at[0]).wait()


def per_device(
    pair,
    single,
    token_valid,
    chain_id,
    w_tri_in,
    w_tri_gate,
    w_tri_out,
    w_att_in,
    w_att_bias,
    w_att_out,
    w_single_in,
    w_pair_bias,
    w_single_out,
):
    vmem = pl.BlockSpec(memory_space=pltpu.VMEM)
    smem = pl.BlockSpec(memory_space=pltpu.SMEM)
    dma = pltpu.SemaphoreType.DMA
    pair_out, single_out = pl.pallas_call(
        pair_kernel,
        out_shape=(
            jax.ShapeDtypeStruct((2048, 128), F32),
            jax.ShapeDtypeStruct((4, 384), F32),
        ),
        in_specs=[vmem] * 4 + [smem] * 2 + [vmem] * 9,
        out_specs=(vmem, vmem),
        scratch_shapes=[
            pltpu.VMEM((512, 128), BF16),
            pltpu.VMEM((128, 128), BF16),
            pltpu.VMEM((128, 128), BF16),
            pltpu.VMEM((128, 128), BF16),
            pltpu.VMEM((2048, 128), F32),
            pltpu.VMEM((2048, 128), F32),
            pltpu.VMEM((128, 32, 128), BF16),
            pltpu.VMEM((128, 32, 128), BF16),
            pltpu.VMEM((8, 128, 256), BF16),
            pltpu.VMEM((8, 128, 256), BF16),
            pltpu.VMEM((8, 8, 256), F32),
            pltpu.VMEM((8, 8, 256), F32),
            pltpu.VMEM((128, 16, 128), BF16),
            pltpu.VMEM((128, 16, 128), BF16),
            pltpu.VMEM((64, 128), BF16),
            pltpu.VMEM((128, 64, 128), BF16),
            pltpu.VMEM((4, 512, 512), F32),
            pltpu.VMEM((4, 512, 128), BF16),
            pltpu.VMEM((4, 128, 512), BF16),
            pltpu.VMEM((4, 512, 256), BF16),
            pltpu.VMEM((4, 512, 128), F32),
            pltpu.VMEM((4, 512, 128), F32),
            pltpu.VMEM((8, 4, 64, 128), BF16),
            pltpu.VMEM((8, 4, 64, 128), BF16),
            pltpu.VMEM((COLS, 16, 128), F32),
            pltpu.VMEM((COLS, 16, 128), F32),
            pltpu.VMEM((16, 128), BF16),
            pltpu.VMEM((128, 16, 128), BF16),
            pltpu.VMEM((1536, 128), F32),
            pltpu.VMEM((512, 384), BF16),
            pltpu.VMEM((512, 384), BF16),
        ]
        + [dma((2,))] * 8,
        compiler_params=pltpu.CompilerParams(
            collective_id=0, has_side_effects=True, vmem_limit_bytes=52 * 1024 * 1024
        ),
    )(
        pair.reshape(2048, 128),
        single,
        token_valid.reshape(4, 128),
        chain_id.reshape(4, 128),
        token_valid,
        chain_id,
        w_tri_in,
        w_tri_gate,
        w_tri_out,
        w_att_in,
        w_att_bias.T,
        w_att_out,
        w_pair_bias.T,
        w_single_in,
        w_single_out,
    )
    return pair_out.reshape(64, 32, 128), single_out


def solution(mesh):
    placed = (P("row", "col", None), P(("row", "col"), None)) + (P(),) * 11
    return jax.shard_map(
        per_device,
        mesh=mesh,
        in_specs=placed,
        out_specs=(P("row", "col", None), P(("row", "col"), None)),
        check_vma=False,
    )
```

time: 715 us -> 120 us (0.17)
  waiting for transfers between devices: 340 us -> 0 us
  blocking collectives: 204 us -> 0 us
  Pallas kernels: 0 us -> 109 us
  local copies, waits for them, and re-layouts: 92.8 us -> 10 us
  matrix products: 40.3 us -> 0 us
  other arithmetic: 20.1 us -> 0 us
  between operations: 14.7 us -> 0.66 us
    all_gather x6 -> x0, waiting for transfers between devices: 263 us -> none  [the longest x1 80.2 us: per_device(): lax.all_gather(right, 'col', axis=1, tiled=True)]
    all_gather x2 -> x0, blocking collectives: 204 us -> none  [the longest x1 177 us: per_device(): single_all = lax.all_gather(single, ('row', 'col'), axis=0, tiled=True)]
    pallas_call x0 -> x1, Pallas kernels: none -> 109 us  [per_device(): pl.pallas_call(pair_kernel, out_shape=(jax.ShapeDtypeStruct((2048, 128),...]
    psum x1 -> x0, waiting for transfers between devices: 75.6 us -> none  [spread_2(): return lax.psum(kept, axis)]
    all_gather x5 -> x0, local copies, waits for them, and re-layouts: 53.4 us -> none  [the longest x1 29.1 us: per_device(): lax.all_gather(left, 'col', axis=1, tiled=True)]
    dot_general x15 -> x0, matrix products: 40.3 us -> none  [the longest x9 11.5 us: project(): jnp.dot(normed.reshape(-1, channel_width), weight, preferred_element_type...]
    reduce_sum x11 -> x0, other arithmetic: 10.6 us -> none  [the longest x1 4.66 us: per_device(): mass = jnp.sum(expo, axis=-1)]
    psum x1 -> x0, local copies, waits for them, and re-layouts: 7.92 us -> none  [spread_2(): return lax.psum(kept, axis)]
  transfers between devices with their start and end apart: 7 -> 0, of which waited for: 6 -> 0; matrix products, arithmetic and copies ran while one was open for 10% -> 0% of each run, Pallas kernels for 0% -> 0%
where the time goes in v1:
time: 120 us
  Pallas kernels  109 us (91%)
  local copies, waits for them, and re-layouts  10 us (8%)
    pallas_call x1, Pallas kernels, per_device(): pl.pallas_call(pair_kernel, out_shape=(jax.ShapeDtypeStruct((2048, 128),...  109 us
    unnamed x24, local copies, waits for them, and re-layouts  10 us

profile of v1, /device:TPU:1, one launch (start us, length us, event | category | flops | bytes accessed | tf_op | source)
XLA Modules:
  0.0 119.7 jit_solution(13601661597253062829)
XLA Ops:
  0.6 0.0 copy-start
  0.6 1.0 copy-done
  1.6 0.0 copy-start.1
  1.6 0.9 copy-done.1
  2.5 0.0 copy-start.2
  2.5 0.9 copy-done.2
  3.4 0.0 copy-start.3
  3.4 0.8 copy-done.3
  4.2 0.0 copy-start.4
  4.2 0.8 copy-done.4
  4.9 0.0 copy-start.5
  4.9 0.8 copy-done.5
  5.7 0.0 copy-start.6
  5.7 0.7 copy-done.6
  6.4 0.0 copy-start.7
  6.4 0.7 copy-done.7
  7.0 0.0 copy-start.8
  7.0 0.7 copy-done.8
  7.7 0.0 copy-start.9
  7.7 0.7 copy-done.9
  8.4 0.0 copy-start.10
  8.4 0.7 copy-done.10
  9.1 109.1 %shard_map.140 = (f32[2048,128]{1,0:T(8,128)S(1)}, f32[4,384]{1,0:T(4,128)S(1)}) custom-call(f32[2048,128]{1,0:T(8,128)} %bitcast.11, bf16[4,384]{1,0:T(4,128)(2,1)S(1)} %copy-done.9, s32[4,128]{1,0:T(4,128)S(1)} %bitcast.7, s32[4,128]{1,0:T(4,128)S(1)} %bitcast.8, s32[512]{0:T(512)S(1)} %copy-done.6, s32[512]{0:T(512)S(1)} %copy-done.7, ...), custom_call_target="tpu_custom_call" | custom-call | tf_op jit(solution)/shard_map/pallas_call | solution.py:498
  118.2 1.0 copy.17
  119.1 0.6 copy.18
Async XLA Ops:
  0.6 1.0 copy-start
  1.6 0.9 copy-start.1
  2.5 0.9 copy-start.2
  3.4 0.8 copy-start.3
  4.2 0.8 copy-start.4
  4.9 0.8 copy-start.5
  5.7 0.7 copy-start.6
  6.4 0.7 copy-start.7
  7.0 0.7 copy-start.8
  7.7 0.7 copy-start.9
  8.4 0.7 copy-start.10

commit v2 on v1

v2 whole, which is shorter than its diff:
```python
import math

import jax
import jax.numpy as jnp
from jax import lax
from jax.experimental import pallas as pl
from jax.experimental.pallas import tpu as pltpu
from jax.sharding import PartitionSpec as P

MESH = pl.DeviceIdType.MESH
F32 = jnp.float32
BF16 = jnp.bfloat16
ROWS = 8
COLS = 16
DEVICES = ROWS * COLS
LOG2E = math.log2(math.e)
EPS = 1e-05


def norm_down(values):
    mean = jnp.mean(values, axis=0, keepdims=True)
    center = values - mean
    spread = jnp.mean(center * center, axis=0, keepdims=True) + EPS
    return center * lax.rsqrt(spread), mean, jnp.sqrt(spread)


def norm_across(values):
    center = values - jnp.mean(values, axis=-1, keepdims=True)
    spread = jnp.mean(center * center, axis=-1, keepdims=True)
    return center * lax.rsqrt(spread + EPS)


def dot(a, b):
    return jnp.dot(a, b, preferred_element_type=F32)


def join_halves(a, b, half):
    first = lax.broadcasted_iota(jnp.int32, a.shape, 1) < 64
    if half == 0:
        return jnp.where(first, a, pltpu.roll(b, 64, 1))
    return jnp.where(first, pltpu.roll(a, 64, 1), b)


def window_kernel(*refs):
    inputs, (out_ref, single_out_ref), scratch = refs[:15], refs[15:17], refs[17:]
    staged, in_sems, scratch = scratch[:15], scratch[15], scratch[16:]
    (
        pair_ref,
        single_ref,
        valid_ref,
        chain_ref,
        valid_smem,
        chain_smem,
        w_tri_in_ref,
        w_tri_gate_ref,
        w_tri_out_ref,
        w_att_in_ref,
        w_att_bias_ref,
        w_att_out_ref,
        w_pair_bias_ref,
        w_single_in_ref,
        w_single_out_ref,
    ) = staged
    (
        w_in_t,
        w_gate_t,
        w_out_t,
        w_key_t,
        w_pair_slots,
        scr_a,
        scr_b,
        lr_send,
        lr_recv,
        norm_send,
        norm_recv,
        stat_send,
        stat_recv,
        prod_send,
        prod_recv,
        bias_send,
        bias_recv,
        bias_full,
        att_t_scr,
        after_scr,
        change_scr,
        query_scr,
        key_scr,
        value_scr,
        gate_scr,
        attended_scr,
        delta_send,
        delta_recv,
        pb_sum,
        pb_send,
        pb_recv,
        single_send,
        single_recv,
        single_scr,
        single_keys,
        single_values,
        lr_sems,
        norm_sems,
        stat_sems,
        prod_sems,
        bias_sems,
        bias_send_sems,
        delta_sems,
        pb_sems,
        single_sems,
    ) = scratch
    loads = [
        pltpu.make_async_copy(inputs[n], staged[n], in_sems.at[n]) for n in range(len(inputs))
    ]
    for load in loads:
        load.start()

    row, col = lax.axis_index("row"), lax.axis_index("col")
    me = row * COLS + col
    group = col * ROWS + row
    core = lax.rem(col, 2)
    partner = col + 1 - 2 * core

    barrier = pltpu.get_barrier_semaphore()

    for row_step in range(ROWS):
        for col_step in range(COLS):
            if row_step or col_step:
                pl.semaphore_signal(
                    barrier,
                    inc=1,
                    device_id=(
                        lax.rem(row + row_step, ROWS),
                        lax.rem(col + col_step, COLS),
                    ),
                    device_id_type=MESH,
                )

    for load in loads:
        load.wait()
    w_in_t[...] = jnp.transpose(w_tri_in_ref[...].astype(F32)).astype(BF16)
    w_gate_t[...] = jnp.transpose(w_tri_gate_ref[...].astype(F32)).astype(BF16)
    w_out_t[...] = jnp.transpose(w_tri_out_ref[...].astype(F32)).astype(BF16)
    lane = lax.broadcasted_iota(jnp.int32, (1, 128), 1)
    valid_pick = valid_ref[pl.ds(row // 2, 1), :].astype(F32)
    valid_row = jnp.where(
        (lane // 64) == lax.rem(row, 2), valid_pick, pltpu.roll(valid_pick, 64, 1)
    )
    for t in range(3):
        single_scr[4 * t : 4 * t + 4, :] = single_ref[:, 128 * t : 128 * t + 128].astype(F32)
    single_scr[12:16, :] = jnp.zeros((4, 128), F32)
    single_send[...] = single_scr[0:16, :].astype(BF16)

    def project_block(step, carry):
        picks = [pair_ref[pl.ds(4 * step + a, 64, stride=32), :] for a in range(4)]
        turned = jnp.transpose(jnp.concatenate(picks, axis=0))
        normed, mean, deviation = norm_down(turned)
        normed = normed.astype(BF16)
        norm_send[step] = normed
        stat_send[step] = jnp.concatenate(
            [jnp.broadcast_to(mean, (4, 256)), jnp.broadcast_to(deviation, (4, 256))], axis=0
        )
        proj = dot(w_in_t[...], normed)
        masks = []
        for s in range(2):
            at = col * 32 + 4 * step + 2 * s
            pick = jnp.where(lane < 64, valid_smem[at], valid_smem[at + 1])
            masks.append(valid_row * pick.astype(F32))
        mask = jnp.concatenate(masks, axis=1)
        left = jax.nn.sigmoid(proj[0:128]) * proj[128:256] * mask
        right = jax.nn.sigmoid(proj[256:384]) * proj[384:512] * mask
        for s in range(2):
            scr_a[pl.ds(2 * step + s, 128, stride=16), :] = left[:, s * 128 : (s + 1) * 128]
            scr_b[pl.ds(2 * step + s, 128, stride=16), :] = right[:, s * 128 : (s + 1) * 128]
        return carry

    lax.fori_loop(0, 8, project_block, 0)
    lr_send[:, 0:16, :] = scr_a[...].reshape(128, 16, 128).astype(BF16)
    lr_send[:, 16:32, :] = scr_b[...].reshape(128, 16, 128).astype(BF16)

    pl.semaphore_wait(barrier, DEVICES - 1)

    def send_lr(step, carry):
        peer = lax.rem(me + step, DEVICES)
        pltpu.make_async_remote_copy(
            src_ref=lr_send.at[peer],
            dst_ref=lr_recv.at[me],
            send_sem=lr_sems.at[0],
            recv_sem=lr_sems.at[1],
            device_id=(peer // COLS, lax.rem(peer, COLS)),
            device_id_type=MESH,
        ).start()
        return carry

    lax.fori_loop(1, DEVICES, send_lr, 0)
    lr_recv[pl.ds(me, 1)] = lr_send[pl.ds(me, 1)]

    def send_single(step, carry):
        peer = lax.rem(row + step, ROWS)
        pltpu.make_async_remote_copy(
            src_ref=single_send,
            dst_ref=single_recv.at[col // 2, core, row],
            send_sem=single_sems.at[0],
            recv_sem=single_sems.at[1],
            device_id=(peer, col),
            device_id_type=MESH,
        ).start()
        return carry

    lax.fori_loop(1, ROWS, send_single, 0)
    single_recv[col // 2, core, row] = single_send[...]

    rest = pl.ds(0, DEVICES - 1)
    pltpu.make_async_copy(lr_send.at[rest], lr_recv.at[rest], lr_sems.at[0]).wait()

    def send_norm(step, carry):
        peer = lax.rem(row + step, ROWS)
        for sent, received, sems in (
            (norm_send, norm_recv, norm_sems),
            (stat_send, stat_recv, stat_sems),
        ):
            pltpu.make_async_remote_copy(
                src_ref=sent.at[peer],
                dst_ref=received.at[row],
                send_sem=sems.at[0],
                recv_sem=sems.at[1],
                device_id=(peer, col),
                device_id_type=MESH,
            ).start()
        return carry

    lax.fori_loop(1, ROWS, send_norm, 0)
    norm_recv[pl.ds(row, 1)] = norm_send[pl.ds(row, 1)]
    stat_recv[pl.ds(row, 1)] = stat_send[pl.ds(row, 1)]

    pltpu.make_async_copy(lr_send.at[rest], lr_recv.at[rest], lr_sems.at[1]).wait()
    left_halves, right_halves = [[], []], [[], []]
    for q in range(4):
        for half in range(2):
            for halves, first in ((left_halves, 0), (right_halves, 16)):
                a = lr_recv[32 * q : 32 * q + 16, first : first + 16, :].reshape(256, 128)
                b = lr_recv[32 * q + 16 : 32 * q + 32, first : first + 16, :].reshape(256, 128)
                halves[half].append(join_halves(a.astype(F32), b.astype(F32), half))
    left_t = jnp.concatenate(
        [jnp.concatenate(left_halves[h], axis=1) for h in range(2)], axis=0
    ).astype(BF16)
    right_t = jnp.concatenate(
        [jnp.concatenate(right_halves[h], axis=1) for h in range(2)], axis=0
    )
    right_all = jnp.transpose(right_t).astype(BF16)
    product = dot(right_all, left_t)
    for ib in range(4):
        scr_a[pl.ds(ib, 512, stride=4), :] = product[:, ib * 128 : (ib + 1) * 128]
    prod_send[...] = scr_a[...].reshape(128, 16, 128).astype(BF16)

    def send_product(step, carry):
        peer = lax.rem(me + step, DEVICES)
        peer_row, peer_col = peer // COLS, lax.rem(peer, COLS)
        pltpu.make_async_remote_copy(
            src_ref=prod_send.at[peer_col * ROWS + peer_row],
            dst_ref=prod_recv.at[me],
            send_sem=prod_sems.at[0],
            recv_sem=prod_sems.at[1],
            device_id=(peer_row, peer_col),
            device_id_type=MESH,
        ).start()
        return carry

    lax.fori_loop(1, DEVICES, send_product, 0)
    prod_recv[pl.ds(me, 1)] = prod_send[pl.ds(group, 1)]

    seven = pl.ds(0, ROWS - 1)
    pltpu.make_async_copy(norm_send.at[seven], norm_recv.at[seven], norm_sems.at[1]).wait()
    pltpu.make_async_copy(stat_send.at[seven], stat_recv.at[seven], stat_sems.at[1]).wait()
    pltpu.make_async_copy(prod_send.at[rest], prod_recv.at[rest], prod_sems.at[1]).wait()

    scr_b[...] = prod_recv[...].reshape(2048, 128).astype(F32)
    valid_all = jnp.concatenate([valid_ref[a : a + 1, :] for a in range(4)], axis=1)
    key_mask = (valid_all.astype(F32) - 1.0) * 10000.0
    for jj in range(4):
        at = slice(64 * (jj // 2) * 2, 64 * (jj // 2) * 2 + 128)
        half = jj % 2
        normed = jnp.concatenate(
            [
                join_halves(
                    norm_recv[2 * ib, :, at].astype(F32),
                    norm_recv[2 * ib + 1, :, at].astype(F32),
                    half,
                )
                for ib in range(4)
            ],
            axis=1,
        )
        stats = jnp.concatenate(
            [
                join_halves(stat_recv[2 * ib, :, at], stat_recv[2 * ib + 1, :, at], half)
                for ib in range(4)
            ],
            axis=1,
        )
        received = jnp.concatenate(
            [scr_b[pl.ds(4 * jj + ib, 128, stride=16), :] for ib in range(4)], axis=1
        )
        product_norm, _, _ = norm_down(received)
        gate = jax.nn.sigmoid(dot(w_gate_t[...], normed.astype(BF16)))
        change = gate * dot(w_out_t[...], product_norm.astype(BF16))
        after = normed * stats[4:5] + stats[0:1] + change
        att_t, _, _ = norm_down(after)
        att_bf = att_t.astype(BF16)
        att_t_scr[jj] = att_bf
        after_scr[jj] = after
        change_scr[jj] = change
        bias = lax.dot_general(
            w_att_bias_ref[...], att_bf, (((1,), (0,)), ((), ())), preferred_element_type=F32
        )
        bias = bias + key_mask
        bias = (bias - jnp.max(bias, axis=1, keepdims=True)) * LOG2E
        for kb in range(4):
            scr_a[pl.ds(4 * jj + kb, 4, stride=16), :] = bias[0:4, kb * 128 : (kb + 1) * 128]
    bias_send[...] = scr_a[0:64, :].reshape(4, 16, 128).astype(BF16)

    def send_bias(slot):
        def push(step, carry):
            peer = lax.rem(me + step, DEVICES)
            pltpu.make_async_remote_copy(
                src_ref=bias_send.at[2 * lax.rem(peer, 2) + slot],
                dst_ref=bias_recv.at[slot, group],
                send_sem=bias_send_sems.at[slot],
                recv_sem=bias_sems.at[slot],
                device_id=(peer // COLS, lax.rem(peer, COLS)),
                device_id_type=MESH,
            ).start()
            return carry

        lax.fori_loop(1, DEVICES, push, 0)
        bias_recv[slot, group] = bias_send[2 * core + slot]

    def bias_left(slot):
        pltpu.make_async_copy(
            bias_recv.at[slot, rest], bias_recv.at[slot, rest], bias_send_sems.at[slot]
        ).wait()

    send_bias(0)

    w_key_t[...] = jnp.transpose(w_att_in_ref[:, 128:256].astype(F32)).astype(BF16)
    w_qvg = jnp.concatenate([w_att_in_ref[:, 0:128], w_att_in_ref[:, 256:512]], axis=1)

    for jj in range(4):
        att_bf = att_t_scr[jj]
        key_scr[jj] = dot(w_key_t[...], att_bf).astype(BF16)
        qvg = dot(jnp.transpose(att_bf.astype(F32)).astype(BF16), w_qvg)
        query_scr[jj] = (qvg[:, 0:128] * (LOG2E / math.sqrt(32.0))).astype(BF16)
        value_scr[jj, :, 0:128] = qvg[:, 128:256].astype(BF16)
        value_scr[jj, :, 128:256] = jnp.ones((512, 128), BF16)
        gate_scr[jj] = jax.nn.sigmoid(qvg[:, 256:384])
    padded = jnp.concatenate(
        [w_pair_bias_ref[...].astype(F32), jnp.zeros((112, 128), F32)], axis=0
    )
    w_pair = jnp.transpose(padded)
    for slot in range(8):
        moved = pltpu.roll(w_pair, 16 * slot, 1) if slot else w_pair
        w_pair_slots[slot] = moved.astype(BF16)
    pb_sum[...] = jnp.zeros((2, 128, 128), F32)

    across = lax.broadcasted_iota(jnp.int32, (128, 128), 1) // 32
    down = lax.broadcasted_iota(jnp.int32, (128, 512), 0) // 32

    def attend(slot, head, begins, ends):
        scr_b[...] = bias_recv[slot].reshape(2048, 128).astype(F32)
        for kb in range(4):
            bias_full[:, kb * 128 : (kb + 1) * 128] = scr_b[pl.ds(kb, 512, stride=4), :]

        for jj in range(4):
            keys = jnp.where(down == head, key_scr[jj].astype(F32), 0.0).astype(BF16)
            if ends:
                after_tok = jnp.transpose(after_scr[jj])
                change_tok = jnp.transpose(change_scr[jj])
            for ib in range(4):
                span = slice(128 * ib, 128 * ib + 128)
                scores = dot(query_scr[jj, span, :], keys) + bias_full[span, :]
                weights = jnp.exp2(scores - jnp.max(scores, axis=1, keepdims=True)).astype(BF16)
                summed = dot(weights, value_scr[jj])
                before = 0.0 if begins else attended_scr[jj, span, :]
                attended = jnp.where(across == head, summed[:, 0:128] / summed[:, 128:256], before)
                if not ends:
                    attended_scr[jj, span, :] = attended
                    continue
                tri_out = (gate_scr[jj, span, :] * attended).astype(BF16)
                added = dot(tri_out, w_att_out_ref[...])
                delta = (change_tok[span] + added).astype(BF16)
                delta_send[2 * ib, pl.ds(jj, 1)] = delta[0:64].reshape(1, 64, 128)
                delta_send[2 * ib + 1, pl.ds(jj, 1)] = delta[64:128].reshape(1, 64, 128)
                scr_a[span, :] = after_tok[span] + added
            if ends:

                def send_delta(step, carry, jj=jj):
                    peer = lax.rem(row + step, ROWS)
                    pltpu.make_async_remote_copy(
                        src_ref=delta_send.at[peer, jj],
                        dst_ref=delta_recv.at[row, jj],
                        send_sem=delta_sems.at[0],
                        recv_sem=delta_sems.at[1],
                        device_id=(peer, col),
                        device_id_type=MESH,
                    ).start()
                    return carry

                lax.fori_loop(1, ROWS, send_delta, 0)
                total = pb_sum[jj // 2]
                for a in range(4):
                    normed = norm_across(scr_a[pl.ds(a, 128, stride=4), :]).astype(BF16)
                    total = total + dot(normed, w_pair_slots[4 * (jj % 2) + a])
                pb_sum[jj // 2] = total

    def hand_on(slot):
        return pltpu.make_async_remote_copy(
            src_ref=bias_recv.at[slot],
            dst_ref=bias_recv.at[2 + slot],
            send_sem=bias_send_sems.at[2 + slot],
            recv_sem=bias_sems.at[2 + slot],
            device_id=(row, partner),
            device_id_type=MESH,
        )

    def gathered(slot):
        pltpu.make_async_copy(
            bias_recv.at[slot, rest], bias_recv.at[slot, rest], bias_sems.at[slot]
        ).wait()

    bias_left(0)
    send_bias(1)
    gathered(0)
    hand_on(0).start()
    pltpu.make_async_copy(
        single_recv.at[0, 0, seven], single_recv.at[0, 0, seven], single_sems.at[1]
    ).wait()

    def spread_single(step, carry):
        peer = lax.rem(col + 2 * step, COLS)
        pltpu.make_async_remote_copy(
            src_ref=single_recv.at[col // 2, core],
            dst_ref=single_recv.at[col // 2, core],
            send_sem=single_sems.at[2],
            recv_sem=single_sems.at[3],
            device_id=(row, peer),
            device_id_type=MESH,
        ).start()
        return carry

    lax.fori_loop(1, COLS // 2, spread_single, 0)
    attend(0, 2 * core, True, False)
    hand_on(0).wait_recv()
    attend(2, 2 * (1 - core), False, False)
    gathered(1)
    hand_on(1).start()
    pltpu.make_async_copy(
        single_recv.at[seven, 0], single_recv.at[seven, 0], single_sems.at[3]
    ).wait()
    pltpu.make_async_remote_copy(
        src_ref=single_recv.at[:, core],
        dst_ref=single_recv.at[:, core],
        send_sem=single_sems.at[4],
        recv_sem=single_sems.at[5],
        device_id=(row, partner),
        device_id_type=MESH,
    ).start()
    attend(1, 2 * core + 1, False, False)
    hand_on(1).wait_recv()
    attend(3, 2 * (1 - core) + 1, False, True)

    for u in range(2):
        pb_send[:, u, :] = pb_sum[u]

    def send_pb(step, carry):
        peer = lax.rem(me + step, DEVICES)
        pltpu.make_async_remote_copy(
            src_ref=pb_send.at[peer],
            dst_ref=pb_recv.at[group],
            send_sem=pb_sems.at[0],
            recv_sem=pb_sems.at[1],
            device_id=(peer // COLS, lax.rem(peer, COLS)),
            device_id_type=MESH,
        ).start()
        return carry

    lax.fori_loop(1, DEVICES, send_pb, 0)
    pb_recv[pl.ds(group, 1)] = pb_send[pl.ds(me, 1)]
    pltpu.make_async_copy(
        single_recv.at[:, core], single_recv.at[:, 1 - core], single_sems.at[5]
    ).wait()
    scr_b[...] = single_recv[...].reshape(2048, 128).astype(F32)
    for t in range(3):
        for a in range(4):
            for r in range(ROWS):
                single_scr[512 * t + 128 * a + 16 * r : 512 * t + 128 * a + 16 * r + 16, :] = scr_b[
                    pl.ds(16 * r + 4 * t + a, 16, stride=128), :
                ]
    single_all = jnp.concatenate(
        [single_scr[512 * t : 512 * t + 512, :] for t in range(3)], axis=1
    )
    single_norm = norm_across(single_all).astype(BF16)
    single_keys[...] = dot(single_norm, w_single_in_ref[:, 384:768]).astype(BF16)
    single_values[...] = dot(single_norm, w_single_in_ref[:, 768:1152]).astype(BF16)

    delta_recv[pl.ds(row, 1)] = delta_send[pl.ds(row, 1)]
    pltpu.make_async_copy(delta_send.at[seven], delta_recv.at[seven], delta_sems.at[1]).wait()

    for k in range(32):
        at = pl.ds(k, 64, stride=32)
        out_ref[at, :] = pair_ref[at, :] + delta_recv[k // 4, k % 4].astype(F32)
    pltpu.make_async_copy(pb_send.at[rest], pb_recv.at[rest], pb_sems.at[1]).wait()

    chain_all = jnp.concatenate([chain_ref[a : a + 1, :] for a in range(4)], axis=1)
    source = lax.broadcasted_iota(jnp.int32, (512, 512), 0)
    place = lax.broadcasted_iota(jnp.int32, (512, 512), 1)
    order = jnp.where(source == 4 * (place % 128) + place // 128, 1.0, 0.0).astype(BF16)
    traits = jnp.concatenate([chain_all, valid_all, jnp.zeros((6, 512), jnp.int32)], axis=0)
    ordered = dot(traits.astype(F32).astype(BF16), order)
    turned = [jnp.transpose(pb_recv[:, u, :]) for u in range(2)]
    pair_bias = jnp.concatenate(
        [turned[jj // 2][64 * (jj % 2) : 64 * (jj % 2) + 64] for jj in range(4)], axis=1
    )
    own = single_ref[...].astype(F32)
    own_norm = norm_across(own).astype(BF16)
    queries = dot(own_norm, w_single_in_ref[:, 0:384]).astype(BF16).astype(F32)
    gate = jax.nn.sigmoid(dot(own_norm, w_single_in_ref[:, 1152:1536]))
    head = lax.broadcasted_iota(jnp.int32, (16, 384), 0) * 24
    channel = lax.broadcasted_iota(jnp.int32, (16, 384), 1)
    mine = (channel >= head) & (channel < head + 24)
    stacked = jnp.concatenate(
        [jnp.where(mine, jnp.broadcast_to(queries[a : a + 1], (16, 384)), 0.0) for a in range(4)],
        axis=0,
    ).astype(BF16)
    scores = lax.dot_general(
        stacked, single_keys[...], (((1,), (1,)), ((), ())), preferred_element_type=F32
    ) * (1.0 / math.sqrt(24.0))
    masks = []
    for a in range(4):
        own_chain = chain_smem[4 * me + a].astype(F32)
        allowed = (ordered[0:1] == own_chain) & (ordered[1:2] == 1.0)
        masks.append(jnp.broadcast_to(jnp.where(allowed, 0.0, -10000.0), (16, 512)))
    scores = scores + pair_bias + jnp.concatenate(masks, axis=0)
    expo = jnp.exp(scores - jnp.max(scores, axis=1, keepdims=True))
    mass = jnp.sum(expo, axis=1, keepdims=True)
    summed = dot(expo.astype(BF16), single_values[...]) / mass
    attended = jnp.concatenate(
        [
            jnp.sum(jnp.where(mine, summed[16 * a : 16 * a + 16], 0.0), axis=0, keepdims=True)
            for a in range(4)
        ],
        axis=0,
    )
    single_out_ref[...] = own + dot((gate * attended).astype(BF16), w_single_out_ref[...])

    pltpu.make_async_copy(norm_send.at[seven], norm_recv.at[seven], norm_sems.at[0]).wait()
    pltpu.make_async_copy(stat_send.at[seven], stat_recv.at[seven], stat_sems.at[0]).wait()
    pltpu.make_async_copy(prod_send.at[rest], prod_recv.at[rest], prod_sems.at[0]).wait()
    bias_left(1)
    for slot in range(2):
        hand_on(slot).wait_send()
    pltpu.make_async_copy(delta_send.at[seven], delta_recv.at[seven], delta_sems.at[0]).wait()
    pltpu.make_async_copy(pb_send.at[rest], pb_recv.at[rest], pb_sems.at[0]).wait()
    pltpu.make_async_copy(
        single_recv.at[0, 0, seven], single_recv.at[0, 0, seven], single_sems.at[0]
    ).wait()
    pltpu.make_async_copy(
        single_recv.at[seven, 0], single_recv.at[seven, 0], single_sems.at[2]
    ).wait()
    pltpu.make_async_copy(
        single_recv.at[:, core], single_recv.at[:, 1 - core], single_sems.at[4]
    ).wait()


def per_device(
    pair,
    single,
    token_valid,
    chain_id,
    w_tri_in,
    w_tri_gate,
    w_tri_out,
    w_att_in,
    w_att_bias,
    w_att_out,
    w_single_in,
    w_pair_bias,
    w_single_out,
):
    vmem = pl.BlockSpec(memory_space=pltpu.VMEM)
    inputs = (
        pair.reshape(2048, 128),
        single,
        token_valid.reshape(4, 128),
        chain_id.reshape(4, 128),
        token_valid,
        chain_id,
        w_tri_in,
        w_tri_gate,
        w_tri_out,
        w_att_in,
        w_att_bias.T,
        w_att_out,
        w_pair_bias.T,
        w_single_in,
        w_single_out,
    )
    dma = pltpu.SemaphoreType.DMA
    staged = [
        pltpu.SMEM(x.shape, x.dtype) if x.ndim == 1 else pltpu.VMEM(x.shape, x.dtype)
        for x in inputs
    ]
    pair_out, single_out = pl.pallas_call(
        window_kernel,
        out_shape=(
            jax.ShapeDtypeStruct((2048, 128), F32),
            jax.ShapeDtypeStruct((4, 384), F32),
        ),
        in_specs=[pl.BlockSpec(memory_space=pltpu.HBM)] * len(inputs),
        out_specs=(vmem, vmem),
        scratch_shapes=staged
        + [
            dma((len(inputs),)),
            pltpu.VMEM((512, 128), BF16),
            pltpu.VMEM((128, 128), BF16),
            pltpu.VMEM((128, 128), BF16),
            pltpu.VMEM((128, 128), BF16),
            pltpu.VMEM((8, 128, 128), BF16),
            pltpu.VMEM((2048, 128), F32),
            pltpu.VMEM((2048, 128), F32),
            pltpu.VMEM((128, 32, 128), BF16),
            pltpu.VMEM((128, 32, 128), BF16),
            pltpu.VMEM((8, 128, 256), BF16),
            pltpu.VMEM((8, 128, 256), BF16),
            pltpu.VMEM((8, 8, 256), F32),
            pltpu.VMEM((8, 8, 256), F32),
            pltpu.VMEM((128, 16, 128), BF16),
            pltpu.VMEM((128, 16, 128), BF16),
            pltpu.VMEM((4, 16, 128), BF16),
            pltpu.VMEM((4, 128, 16, 128), BF16),
            pltpu.VMEM((512, 512), F32),
            pltpu.VMEM((4, 128, 512), BF16),
            pltpu.VMEM((4, 128, 512), F32),
            pltpu.VMEM((4, 128, 512), F32),
            pltpu.VMEM((4, 512, 128), BF16),
            pltpu.VMEM((4, 128, 512), BF16),
            pltpu.VMEM((4, 512, 256), BF16),
            pltpu.VMEM((4, 512, 128), F32),
            pltpu.VMEM((4, 512, 128), F32),
            pltpu.VMEM((8, 4, 64, 128), BF16),
            pltpu.VMEM((8, 4, 64, 128), BF16),
            pltpu.VMEM((2, 128, 128), F32),
            pltpu.VMEM((128, 2, 128), F32),
            pltpu.VMEM((128, 2, 128), F32),
            pltpu.VMEM((16, 128), BF16),
            pltpu.VMEM((8, 2, 8, 16, 128), BF16),
            pltpu.VMEM((1536, 128), F32),
            pltpu.VMEM((512, 384), BF16),
            pltpu.VMEM((512, 384), BF16),
            dma((2,)),
            dma((2,)),
            dma((2,)),
            dma((2,)),
            dma((4,)),
            dma((4,)),
            dma((2,)),
            dma((2,)),
            dma((6,)),
        ],
        compiler_params=pltpu.CompilerParams(
            collective_id=0, has_side_effects=True, vmem_limit_bytes=58 * 1024 * 1024
        ),
    )(*inputs)
    return pair_out.reshape(64, 32, 128), single_out


def solution(mesh):
    placed = (P("row", "col", None), P(("row", "col"), None)) + (P(),) * 11
    return jax.shard_map(
        per_device,
        mesh=mesh,
        in_specs=placed,
        out_specs=(P("row", "col", None), P(("row", "col"), None)),
        check_vma=False,
    )
```

time: 120 us -> 85.9 us (0.72)
  Pallas kernels: 109 us -> 82.2 us
  local copies, waits for them, and re-layouts: 10 us -> 2.87 us
    pallas_call x1, Pallas kernels: 109 us -> 82.2 us  [per_device(): pl.pallas_call(window_kernel, out_shape=(jax.ShapeDtypeStruct((2048, 128)...]
    unnamed x24 -> x4, local copies, waits for them, and re-layouts: 10 us -> 2.87 us
where the time goes in v2:
time: 85.9 us; the launch traced here: 85.7 us
  Pallas kernels  82.2 us (96%)
  local copies, waits for them, and re-layouts  2.87 us (3%)
    pallas_call x1, Pallas kernels, per_device(): pl.pallas_call(window_kernel, out_shape=(jax.ShapeDtypeStruct((2048, 128)...  82.2 us
    unnamed x4, local copies, waits for them, and re-layouts  2.87 us

profile of v2, /device:TPU:1, one launch (start us, length us, event | category | flops | bytes accessed | tf_op | source)
XLA Modules:
  0.0 85.7 jit_solution(10148716478135442822)
XLA Ops:
  0.6 82.2 %shard_map.140 = (f32[2048,128]{1,0:T(8,128)}, f32[4,384]{1,0:T(4,128)}) custom-call(f32[2048,128]{1,0:T(8,128)} %bitcast.7, bf16[4,384]{1,0:T(4,128)(2,1)} %refs_1_.1, s32[4,128]{1,0:T(4,128)} %bitcast.8, s32[4,128]{1,0:T(4,128)} %bitcast.9, s32[512]{0:T(512)} %refs_4_.1, s32[512]{0:T(512)} %refs_5_.1, bf16[128,512]{1,0:T(8,128)(2,1)} %refs_6_.1, ...), custom_call_target="tpu_custom_call" | custom-call | tf_op jit(solution)/shard_map/pallas_call | solution.py:611
  82.8 0.0 copy-start
  82.8 2.3 %copy.17 = f32[64,32,128]{2,1,0:T(8,128)} copy(f32[64,32,128]{2,1,0:T(8,128)} %bitcast.6) | data formatting | bytes 2097152
  85.1 0.0 copy-done
  85.1 0.6 copy.18
Async XLA Ops:
  82.8 2.3 %copy-start = (f32[4,384]{1,0:T(4,128)S(1)}, f32[4,384]{1,0:T(4,128)}, u32[]{:S(2)}) copy-start(f32[4,384]{1,0:T(4,128)} %get-tuple-element.9) | copy-start | bytes 18436

commit v3 on v2

--- a/solution.py
+++ b/solution.py
@@ -501,24 +501,12 @@
     single_keys[...] = dot(single_norm, w_single_in_ref[:, 384:768]).astype(BF16)
     single_values[...] = dot(single_norm, w_single_in_ref[:, 768:1152]).astype(BF16)
 
-    delta_recv[pl.ds(row, 1)] = delta_send[pl.ds(row, 1)]
-    pltpu.make_async_copy(delta_send.at[seven], delta_recv.at[seven], delta_sems.at[1]).wait()
-
-    for k in range(32):
-        at = pl.ds(k, 64, stride=32)
-        out_ref[at, :] = pair_ref[at, :] + delta_recv[k // 4, k % 4].astype(F32)
-    pltpu.make_async_copy(pb_send.at[rest], pb_recv.at[rest], pb_sems.at[1]).wait()
-
     chain_all = jnp.concatenate([chain_ref[a : a + 1, :] for a in range(4)], axis=1)
     source = lax.broadcasted_iota(jnp.int32, (512, 512), 0)
     place = lax.broadcasted_iota(jnp.int32, (512, 512), 1)
     order = jnp.where(source == 4 * (place % 128) + place // 128, 1.0, 0.0).astype(BF16)
     traits = jnp.concatenate([chain_all, valid_all, jnp.zeros((6, 512), jnp.int32)], axis=0)
     ordered = dot(traits.astype(F32).astype(BF16), order)
-    turned = [jnp.transpose(pb_recv[:, u, :]) for u in range(2)]
-    pair_bias = jnp.concatenate(
-        [turned[jj // 2][64 * (jj % 2) : 64 * (jj % 2) + 64] for jj in range(4)], axis=1
-    )
     own = single_ref[...].astype(F32)
     own_norm = norm_across(own).astype(BF16)
     queries = dot(own_norm, w_single_in_ref[:, 0:384]).astype(BF16).astype(F32)
@@ -538,6 +526,19 @@
         own_chain = chain_smem[4 * me + a].astype(F32)
         allowed = (ordered[0:1] == own_chain) & (ordered[1:2] == 1.0)
         masks.append(jnp.broadcast_to(jnp.where(allowed, 0.0, -10000.0), (16, 512)))
+
+    delta_recv[pl.ds(row, 1)] = delta_send[pl.ds(row, 1)]
+    pltpu.make_async_copy(delta_send.at[seven], delta_recv.at[seven], delta_sems.at[1]).wait()
+
+    for k in range(32):
+        at = pl.ds(k, 64, stride=32)
+        out_ref[at, :] = pair_ref[at, :] + delta_recv[k // 4, k % 4].astype(F32)
+    pltpu.make_async_copy(pb_send.at[rest], pb_recv.at[rest], pb_sems.at[1]).wait()
+
+    turned = [jnp.transpose(pb_recv[:, u, :]) for u in range(2)]
+    pair_bias = jnp.concatenate(
+        [turned[jj // 2][64 * (jj % 2) : 64 * (jj % 2) + 64] for jj in range(4)], axis=1
+    )
     scores = scores + pair_bias + jnp.concatenate(masks, axis=0)
     expo = jnp.exp(scores - jnp.max(scores, axis=1, keepdims=True))
     mass = jnp.sum(expo, axis=1, keepdims=True)

time: 85.9 us -> 85.5 us (level)
  no operation moved by 1% of the time
where the time goes in v3:
time: 85.5 us; the launch traced here: 85.3 us
  Pallas kernels  81.8 us (96%)
  local copies, waits for them, and re-layouts  2.87 us (3%)
    pallas_call x1, Pallas kernels, per_device(): pl.pallas_call(window_kernel, out_shape=(jax.ShapeDtypeStruct((2048, 128)...  81.8 us
    unnamed x4, local copies, waits for them, and re-layouts  2.87 us

profile of v3, /device:TPU:1, one launch (start us, length us, event | category | flops | bytes accessed | tf_op | source)
XLA Modules:
  0.0 85.3 jit_solution(7310974702281638174)
XLA Ops:
  0.6 81.8 %shard_map.140 = (f32[2048,128]{1,0:T(8,128)}, f32[4,384]{1,0:T(4,128)}) custom-call(f32[2048,128]{1,0:T(8,128)} %bitcast.7, bf16[4,384]{1,0:T(4,128)(2,1)} %refs_1_.1, s32[4,128]{1,0:T(4,128)} %bitcast.8, s32[4,128]{1,0:T(4,128)} %bitcast.9, s32[512]{0:T(512)} %refs_4_.1, s32[512]{0:T(512)} %refs_5_.1, bf16[128,512]{1,0:T(8,128)(2,1)} %refs_6_.1, ...), custom_call_target="tpu_custom_call" | custom-call | tf_op jit(solution)/shard_map/pallas_call | solution.py:612
  82.5 0.0 copy-start
  82.5 2.3 %copy.17 = f32[64,32,128]{2,1,0:T(8,128)} copy(f32[64,32,128]{2,1,0:T(8,128)} %bitcast.6) | data formatting | bytes 2097152
  84.7 0.0 copy-done
  84.7 0.6 copy.18
Async XLA Ops:
  82.5 2.3 %copy-start = (f32[4,384]{1,0:T(4,128)S(1)}, f32[4,384]{1,0:T(4,128)}, u32[]{:S(2)}) copy-start(f32[4,384]{1,0:T(4,128)} %get-tuple-element.9) | copy-start | bytes 18436
